TPU v7x, 32 devices: a whole 2x2x4 slice. The times are simulated.
32 devices in a mesh: groups: 2 (over x), expert: 16 (over z, y, core).
Axes of the slice: x: 2, y: 2, z: 4, core: 2. Of those that a mesh axis runs over, the one named last changes fastest.
Arguments:
- residual: bfloat16 [64, 7168], P(('groups', 'expert')), parts along dimension 0, may hold values from -6 to 6
- attention: bfloat16 [64, 2048], P('groups', 'expert'), parts along dimension 0, may hold values from -6 to 6
- out_weight: bfloat16 [2048, 7168], P('expert'), may hold values from -0.125 to 0.125
- norm_gain: float32 [7168], replicated, may hold values from 0.1 to 1.9
- route_ids: int32 [64, 2], P(('groups', 'expert')), parts along dimension 0, may hold values from 0 to 3, all different within a row; in each aligned block of 2 rows (0 to 1, 2 to 3, ...) at most 2 rows name the same one
- route_weight: float32 [64, 2], P(('groups', 'expert')), parts along dimension 0, may hold values from 0.2 to 1
- gate_weight: bfloat16 [16, 7168, 256], P('expert'), may hold values from -0.0625 to 0.0625
- up_weight: bfloat16 [16, 7168, 256], P('expert'), may hold values from -0.0625 to 0.0625
- down_weight: bfloat16 [16, 256, 7168], P('expert'), may hold values from -0.1875 to 0.1875
Outputs:
- mixed: bfloat16 [64, 7168], P(('groups', 'expert')), parts along dimension 0
There are 2 independent parts, one for each index of `groups`. A program takes and returns all parts, laid end to end along the dimension named above; an argument that names none is the same for every part. Nothing has to cross between parts.
Inputs may be any that keep to these rules, and one draw needn't show every extreme that they name: `route_ids`: each row names 2 different experts. In each aligned block of 2 rows (the rows of one device) no expert is named by more than 2 rows, and in some block one expert is named by exactly 2 rows.
All inputs are finite; a program needn't handle non-finite values.
Results may differ from a plain program's by a relative error of at most 0.0038.
Values may be sent and summed in bfloat16 or wider, within the bound.
A program may use at most 64 MiB of HBM per device.

v0:
```python
import jax
import jax.numpy as jnp
from jax import lax
from jax.sharding import PartitionSpec as P

FF_WIN = 1024


EPSILON = 1e-06


def expert_partial(in_rows, w_gate, w_up, w_down):
    in_shape = in_rows.shape
    flat_rows = in_rows.reshape(-1, in_shape[-1])
    gate_out = jnp.dot(flat_rows, w_gate[0], preferred_element_type=jnp.float32)
    up_out = jnp.dot(flat_rows, w_up[0], preferred_element_type=jnp.float32)
    activated = (jax.nn.silu(gate_out) * up_out).astype(jnp.bfloat16)
    partial_out = jnp.dot(activated, w_down[0], preferred_element_type=jnp.float32).astype(
        jnp.bfloat16
    )
    return partial_out.reshape(in_shape[:-1] + (w_down.shape[2],))


def local(
    residual,
    attention,
    out_weight,
    norm_gain,
    route_ids,
    route_weight,
    gate_weight,
    up_weight,
    down_weight,
):
    tok_rows, model_width = residual.shape
    top_count = route_ids.shape[1]
    devices = lax.axis_size("expert")
    split_count = FF_WIN // gate_weight.shape[2]
    expert_count = devices // split_count
    capacity = max(2, 2 * tok_rows * top_count // expert_count)
    slot_total = expert_count * capacity
    hidden_state = residual.astype(jnp.float32) + lax.psum_scatter(
        jnp.dot(attention, out_weight, preferred_element_type=jnp.float32),
        "expert",
        scatter_dimension=0,
        tiled=True,
    )
    inv_rms = lax.rsqrt(jnp.mean(hidden_state * hidden_state, axis=-1, keepdims=True) + EPSILON)
    normed = (hidden_state * inv_rms * norm_gain).astype(jnp.bfloat16)
    flat_ids = route_ids.reshape(-1)
    onehot = (flat_ids[:, None] == jnp.arange(expert_count, dtype=jnp.int32)[None, :]).astype(
        jnp.int32
    )
    earlier = jnp.cumsum(onehot, axis=0) - onehot
    slot_of = jnp.sum(earlier * onehot, axis=1)
    position = flat_ids * capacity + slot_of
    selector = (position[:, None] == jnp.arange(slot_total, dtype=jnp.int32)[None, :]).astype(
        jnp.float32
    )
    selector = selector.reshape(tok_rows, top_count, slot_total)
    placing = jnp.sum(selector, axis=1).astype(jnp.bfloat16)
    combine_weights = jnp.sum(selector * route_weight[:, :, None], axis=1)
    outgoing = jnp.einsum("ts,td->sd", placing, normed, preferred_element_type=jnp.float32).astype(
        jnp.bfloat16
    )
    outgoing = outgoing.reshape(expert_count, capacity, model_width)
    copies = jnp.broadcast_to(outgoing[:, None], (expert_count, split_count, capacity, model_width))
    copies = copies.reshape(devices, capacity, model_width)
    partial_out = expert_partial(
        lax.all_to_all(copies, "expert", split_axis=0, concat_axis=0, tiled=True),
        gate_weight,
        up_weight,
        down_weight,
    )
    returned = lax.all_to_all(partial_out, "expert", split_axis=0, concat_axis=0, tiled=True)
    returned = returned.reshape(expert_count, split_count, capacity, model_width)
    expert_out = jnp.sum(returned.astype(jnp.float32), axis=1)
    mixed = hidden_state + jnp.dot(
        combine_weights,
        expert_out.reshape(slot_total, model_width),
        precision=lax.Precision.HIGHEST,
        preferred_element_type=jnp.float32,
    )
    return mixed.astype(jnp.bfloat16)


def solution(mesh):
    return jax.shard_map(
        local,
        mesh=mesh,
        in_specs=(
            P(("groups", "expert"), None),
            P("groups", "expert"),
            P("expert", None),
            P(),
            P(("groups", "expert"), None),
            P(("groups", "expert"), None),
            P("expert", None, None),
            P("expert", None, None),
            P("expert", None, None),
        ),
        out_specs=P(("groups", "expert"), None),
        check_vma=False,
    )
```

profile of v0, /device:TPU:0, one launch (start us, length us, event | category | flops | bytes accessed | tf_op | source)
XLA Modules:
  0.0 160.9 jit_solution(4677015993802672419)
XLA Ops:
  6.5 0.0 copy-start
  6.6 0.0 all-reduce.3.cloned.1.call-start
  6.6 1.4 copy-done
  8.1 2.0 %fusion.24 = f32[32,7168]{1,0:T(8,128)} fusion(bf16[32,128]{1,0:T(8,128)(2,1)} %param.10, bf16[128,7168]{1,0:T(8,128)(2,1)S(1)} %copy-done), kind=kOutput, calls=%fused_computation.32 | convolution fusion | flops 58720256 | bytes 2760704 | tf_op jit(solution)/shard_map/dot_general | solution.py:43
  10.1 0.0 all-reduce.3.cloned.1.call-update
  10.1 0.1 eq.29
  10.2 0.1 fusion.21
  10.3 0.2 select_reduce_fusion.1
  10.5 0.1 reduce_sum.48
  10.6 0.6 dynamic-slice
  11.9 0.1 convert_reduce_fusion.1
  11.9 93.6 %all-reduce.3.cloned.1.call-done = f32[32,7168]{1,0:T(8,128)} async-done(((f32[32,7168]{1,0:T(8,128)}), f32[32,7168]{1,0:T(8,128)}) %all-reduce.3.cloned.1.call-update) | async-done | bytes 917520
  105.5 1.1 multiply_reduce_fusion
  106.6 1.2 convolution_convert_fusion.1
  107.9 0.2 broadcast_in_dim.5
  108.1 18.1 %all_to_all.10 = bf16[16,2,7168]{2,1,0:T(2,128)(2,1)S(1)} all-to-all(bf16[16,2,7168]{2,1,0:T(2,128)(2,1)S(1)} %bitcast.27), channel_id=1, replica_groups=mesh['groups'=2,'expert'=16] {'expert'}, dimensions={0} | all-to-all | bytes 917504 | tf_op jit(solution)/shard_map/all_to_all | solution.py:70
  126.2 0.2 reshape.46
  126.4 2.8 %fusion.4 = f32[32,256]{1,0:T(8,128)S(1)} fusion(bf16[32,7168]{1,0:T(8,128)(2,1)S(1)} %reshape.46, bf16[1,7168,256]{2,1,0:T(8,128)(2,1)} %param.15), kind=kOutput, calls=%fused_computation.7 | convolution fusion | flops 117440512 | bytes 4161536 | tf_op jit(solution)/shard_map/dot_general | solution.py:15
  129.2 5.2 %convolution_convert_fusion = bf16[32,7168]{1,0:T(8,128)(2,1)S(1)} fusion(bf16[1,256,7168]{2,1,0:T(8,128)(2,1)} %param.17, bf16[32,7168]{1,0:T(8,128)(2,1)S(1)} %reshape.46, bf16[1,7168,256]{2,1,0:T(8,128)(2,1)} %param.16, f32[32,256]{1,0:T(8,128)S(1)} %fusion.4), kind=kOutput, calls=%fused_computation | convolution fusion | flops 235159552 | bytes 8290304 | tf_op jit(solution)/shard_map/dot_general | solution.py:18
  134.4 0.2 reshape.47
  134.6 16.9 %all_to_all.11 = bf16[16,2,7168]{2,1,0:T(2,128)(2,1)S(1)} all-to-all(bf16[16,2,7168]{2,1,0:T(2,128)(2,1)S(1)} %reshape.47), channel_id=1, replica_groups=mesh['groups'=2,'expert'=16] {'expert'}, dimensions={0} | all-to-all | bytes 917504 | tf_op jit(solution)/shard_map/all_to_all | solution.py:75
  151.5 0.5 convert_reduce_fusion
  152.0 0.2 reshape.48
  152.2 1.9 %fusion = bf16[2,7168]{1,0:T(2,128)(2,1)} fusion(f32[2,8]{1,0:T(2,128)S(1)} %get-tuple-element.6, f32[8,7168]{1,0:T(8,128)S(1)} %reshape.48, f32[32,7168]{1,0:T(8,128)} %all-reduce.3.cloned.1.call-done, u32[]{:T(128)S(6)} %multiply.7, bf16[2,7168]{1,0:T(2,128)(2,1)S(1)} %copy-done.1), kind=kOutput, calls=%fused_computation.3 | convolution fusion | flops 1433600 | bytes 344132 | tf_op jit(solution)/shard_map/dot_general | solution.py:78
  (14 shorter events, 0.1 us)
Async XLA Ops:
  6.5 1.5 copy-start
  6.5 4.1 %copy-start.5 = (u32[32]{0:T(128)S(1)}, u32[32]{0:T(128)}, u32[]{:S(2)}) copy-start(u32[32]{0:T(128)} %constant.27) | copy-start | bytes 388
  6.5 3.6 %copy-start.2 = (s32[2,2]{1,0:T(2,128)S(1)}, s32[2,2]{1,0:T(2,128)}, u32[]{:S(2)}) copy-start(s32[2,2]{1,0:T(2,128)} %param.13) | copy-start | bytes 52
  6.5 5.3 %copy-start.3 = (f32[2,2]{1,0:T(2,128)S(1)}, f32[2,2]{1,0:T(2,128)}, u32[]{:S(2)}) copy-start(f32[2,2]{1,0:T(2,128)} %param.14) | copy-start | bytes 52
  6.5 99.0 %copy-start.1 = (bf16[2,7168]{1,0:T(2,128)(2,1)S(1)}, bf16[2,7168]{1,0:T(2,128)(2,1)}, u32[]{:S(2)}) copy-start(bf16[2,7168]{1,0:T(2,128)(2,1)} %param.9) | copy-start | bytes 86020
  6.5 100.1 %copy-start.4 = (f32[7168]{0:T(1024)S(1)}, f32[7168]{0:T(1024)}, u32[]{:S(2)}) copy-start(f32[7168]{0:T(1024)} %param.12) | copy-start | bytes 86020
  6.6 99.0 %all-reduce.3.cloned.1.call-start = ((), (), s32[]{:S(2)}) async-start(), calls=%async_computation.2 | async-start | bytes 1835008
Sparse Core Ops, SparseCore 0:
  10.9 94.6 all-reduce.2
where the time goes:
time: 161 us
  waiting for transfers between devices  93.6 us (58%)
  blocking collectives  35 us (22%)
  between operations  14.1 us (9%)
  matrix products  13.1 us (8%)
  local copies, waits for them, and re-layouts  3.03 us (2%)
  other arithmetic  1.99 us (1%)
    unnamed x2, waiting for transfers between devices  93.6 us
    all_to_all x1, blocking collectives, local(): lax.all_to_all(copies, 'expert', split_axis=0, concat_axis=0, tiled=True)  18.1 us
    all_to_all x1, blocking collectives, local(): lax.all_to_all(partial_out, 'expert', split_axis=0, concat_axis=0, tiled=...  16.9 us
    dot_general x1, matrix products, expert_partial(): jnp.dot(activated, w_down[0], preferred_element_type=jnp.float32)  5.25 us
  transfers between devices with their start and end apart: 1, of which 1 were waited for; matrix products, arithmetic and copies ran while one was open for 1% of the time, Pallas kernels for 0%

commit v1 on v0

v1 whole, which is shorter than its diff:
```python
import functools

import jax
import jax.numpy as jnp
from jax import lax
from jax.experimental import pallas as pl
from jax.experimental.pallas import tpu as pltpu
from jax.sharding import PartitionSpec as P

FF_WIN = 1024
EPSILON = 1e-06
PIECES = 8
META = 128
CHUNKS = ((0, 512), (512, 384))
MESH = pl.DeviceIdType.MESH


def split_three(value):
    high = value.astype(jnp.bfloat16).astype(jnp.float32)
    rest = value - high
    middle = rest.astype(jnp.bfloat16).astype(jnp.float32)
    return high, middle, rest - middle


def kernel(
    n,
    expert_split,
    residual,
    attention,
    gain,
    route_ids,
    route_weight,
    wo_hbm,
    wg_hbm,
    wu_hbm,
    wd_hbm,
    out,
    wo,
    wg,
    wu,
    wd,
    partial,
    gathered,
    tokens,
    hidden,
    gain_tile,
    meta,
    send_c,
    recv_c,
    send_b,
    recv_b,
    send_a,
    recv_a,
    load_sem,
    c_sem,
    b_sem,
    a_sem,
    gc_sem,
    gb_sem,
    ga_sem,
):
    width = gain_tile.shape[1]
    far = n // 4
    top = route_ids.shape[1]
    steps = range(len(CHUNKS))
    last = len(CHUNKS) - 1
    me = lax.axis_index("expert")
    a, b, c = me // 4, (me // 2) % 2, me % 2
    peer_c, peer_b = me + 1 - 2 * c, me + 2 - 4 * b
    peers_a = [lax.rem(me + 4 * d, n) for d in range(1, far)]

    loads = [
        pltpu.make_async_copy(wo_hbm, wo, load_sem.at[0]),
        pltpu.make_async_copy(wg_hbm.at[0], wg, load_sem.at[1]),
        pltpu.make_async_copy(wu_hbm.at[0], wu, load_sem.at[2]),
        pltpu.make_async_copy(wd_hbm.at[0], wd, load_sem.at[3]),
    ]
    for load in loads:
        load.start()

    barrier = pltpu.get_barrier_semaphore()
    for peer in [peer_c, peer_b] + peers_a:
        pl.semaphore_signal(barrier, inc=1, device_id={"expert": peer}, device_id_type=MESH)

    def remote(src, dst, sems, peer):
        return pltpu.make_async_remote_copy(
            src_ref=src,
            dst_ref=dst,
            send_sem=sems.at[0],
            recv_sem=sems.at[1],
            device_id={"expert": peer},
            device_id_type=MESH,
        )

    def lanes(k):
        return pl.ds(*CHUNKS[k])

    def wide(k):
        start, size = CHUNKS[k]
        return pl.ds(start, size + (META if k == last else 0))

    copies_c = [
        [
            remote(send_c.at[r, :, :, lanes(k)], recv_c.at[r, :, :, lanes(k)], c_sem.at[r, k], peer_c)
            for k in steps
        ]
        for r in range(2)
    ]
    copies_b = [
        [
            remote(send_b.at[r, :, :, lanes(k)], recv_b.at[r, :, :, lanes(k)], b_sem.at[r, k], peer_b)
            for k in steps
        ]
        for r in range(2)
    ]
    copies_a = [
        [
            [
                remote(
                    send_a.at[r, d, :, lanes(k)],
                    recv_a.at[r, d, :, lanes(k)],
                    a_sem.at[r, k, d],
                    peers_a[d],
                )
                for d in range(far - 1)
            ]
            for k in steps
        ]
        for r in range(2)
    ]
    gathers_a = [
        [
            remote(
                gathered.at[a, b, c, :, wide(k)],
                gathered.at[a, b, c, :, wide(k)],
                ga_sem.at[k, d],
                peers_a[d],
            )
            for d in range(far - 1)
        ]
        for k in steps
    ]
    gathers_b = [
        remote(gathered.at[:, b, c, :, wide(k)], gathered.at[:, b, c, :, wide(k)], gb_sem.at[k], peer_b)
        for k in steps
    ]
    gathers_c = [
        remote(gathered.at[:, :, c, :, wide(k)], gathered.at[:, :, c, :, wide(k)], gc_sem.at[k], peer_c)
        for k in steps
    ]

    def block(owner, k):
        start, size = CHUNKS[k]
        return partial[pl.ds(2 * owner, 2), :, start : start + size].reshape(2 * PIECES, size)

    def keep(owner, k, value):
        start, size = CHUNKS[k]
        partial[pl.ds(2 * owner, 2), :, start : start + size] = value.reshape(2, PIECES, size)

    def spread(k, left, right, scale):
        start, size = CHUNKS[k]
        for j in range(PIECES):
            at = j * width + start
            product = jnp.dot(left, right[:, at : at + size], preferred_element_type=jnp.float32)
            partial[:, j, start : start + size] = product if scale is None else product * scale

    def first(r, k):
        start, size = CHUNKS[k]

        @pl.loop(0, 2 * far)
        def _(i):
            value = block(2 * i + 1 - c, k).astype(jnp.bfloat16)
            send_c[r, i, :, start : start + size] = value

    def second(r, k):
        start, size = CHUNKS[k]
        copies_c[r][k].wait_recv()

        def total(i):
            received = recv_c[r, i, :, start : start + size].astype(jnp.float32)
            return block(2 * i + c, k) + received

        @pl.loop(0, far)
        def _(q):
            send_b[r, q, :, start : start + size] = total(2 * q + 1 - b).astype(jnp.bfloat16)

        copies_b[r][k].start()

        @pl.loop(0, far)
        def _(q):
            i = 2 * q + b
            keep(2 * i + c, k, total(i))

    def third(r, k):
        start, size = CHUNKS[k]
        copies_b[r][k].wait_recv()

        def total(q):
            received = recv_b[r, q, :, start : start + size].astype(jnp.float32)
            return block(4 * q + 2 * b + c, k) + received

        for d in range(far - 1):
            value = total(peers_a[d] // 4).astype(jnp.bfloat16)
            send_a[r, d, :, start : start + size] = value
            copies_a[r][k][d].start()
        keep(me, k, total(a))

    def fourth(r, k):
        start, size = CHUNKS[k]
        value = block(me, k)
        for d in range(far - 1):
            copies_a[r][k][d].wait_recv()
            value = value + recv_a[r, d, :, start : start + size].astype(jnp.float32)
        return value.reshape(2, PIECES, size)

    lane = lax.broadcasted_iota(jnp.int32, (1, META), 1)
    meta[...] = jnp.zeros_like(meta)
    for row in range(2):
        coef = jnp.zeros((1, META), jnp.float32)
        for k in range(top):
            chosen = route_ids[row : row + 1, k : k + 1] == lane
            coef = coef + jnp.where(chosen, route_weight[row : row + 1, k : k + 1], 0.0)
        for place, value in enumerate(split_three(coef)):
            meta[row, 3 + place : 4 + place, :] = value
    for j in range(PIECES):
        hidden[:, j, :] = residual[:, j * width : (j + 1) * width].astype(jnp.float32)
        gain_tile[j : j + 1, :] = gain[:, j * width : (j + 1) * width]

    squares = []

    def normed(k):
        start, size = CHUNKS[k]
        value = hidden[:, :, start : start + size] + fourth(0, k)
        hidden[:, :, start : start + size] = value
        scaled = value * gain_tile[:, start : start + size][None]
        gathered[a, b, c, :, start : start + size] = scaled.reshape(2 * PIECES, size).astype(
            jnp.bfloat16
        )
        part = jnp.sum(jnp.sum(value * value, axis=2, keepdims=True), axis=1, keepdims=True)
        squares.append(part)
        if k == last:
            total = sum(squares[1:], squares[0])
            for row in range(2):
                spreaded = jnp.broadcast_to(total[row], (1, META))
                for place, piece in enumerate(split_three(spreaded)):
                    meta[row, place : place + 1, :] = piece
            gathered[a, b, c, :, width:] = meta[...].reshape(2 * PIECES, META).astype(jnp.bfloat16)
        for copy in gathers_a[k]:
            copy.start()

    def pass_b(k):
        for copy in gathers_a[k]:
            copy.wait_recv()
        gathers_b[k].start()

    def pass_c(k):
        gathers_b[k].wait_recv()
        gathers_c[k].start()

    products = []

    def consume(k):
        start, size = CHUNKS[k]
        size_wide = size + (META if k == last else 0)
        gathers_c[k].wait_recv()

        @pl.loop(0, n)
        def _(owner):
            value = gathered[owner // 4, (owner // 2) % 2, owner % 2, :, start : start + size_wide]
            tokens[pl.ds(2 * owner, 2), :, start : start + size_wide] = value.astype(
                jnp.float32
            ).reshape(2, PIECES, size_wide)

        if k == 0:
            loads[1].wait()
            loads[2].wait()
        for j in range(PIECES):
            rows = tokens[:, j, start : start + size].astype(jnp.bfloat16)
            at = j * width + start
            products.append(
                (
                    jnp.dot(rows, wg[at : at + size, :], preferred_element_type=jnp.float32),
                    jnp.dot(rows, wu[at : at + size, :], preferred_element_type=jnp.float32),
                )
            )
            if len(products) > 1:
                later, earlier = products.pop(), products.pop()
                products.append((earlier[0] + later[0], earlier[1] + later[1]))

    def project(k):
        if k == 0:
            loads[0].wait()
        spread(k, attention[...], wo, None)
        first(0, k)
        if k == 0:
            pl.semaphore_wait(barrier, far + 1)
        copies_c[0][k].start()

    stages = [
        project,
        lambda k: second(0, k),
        lambda k: third(0, k),
        normed,
        pass_b,
        pass_c,
        consume,
    ]
    for step in range(len(stages) + last):
        for k in steps:
            if 0 <= step - k < len(stages):
                stages[step - k](k)

    gate, up = products[0]
    mean = (tokens[:, 0, width:] + tokens[:, 1, width:] + tokens[:, 2, width:]) * (
        1.0 / (PIECES * width)
    )
    inv_rms = lax.rsqrt(mean + EPSILON)[:, :1]
    coefs = tokens[:, 3, width:] + tokens[:, 4, width:] + tokens[:, 5, width:]
    coef = jnp.sum(jnp.where(lane == me // expert_split, coefs, 0.0), axis=1, keepdims=True)
    gate, up = gate * inv_rms, up * inv_rms
    act = (gate / (1.0 + jnp.exp(-gate)) * up).astype(jnp.bfloat16)
    loads[3].wait()

    def down(k):
        spread(k, act, wd, coef)
        first(1, k)
        copies_c[1][k].start()

    def final(k):
        start, size = CHUNKS[k]
        hidden[:, :, start : start + size] = hidden[:, :, start : start + size] + fourth(1, k)
        for j in range(PIECES):
            at = j * width + start
            out[:, at : at + size] = hidden[:, j, start : start + size].astype(out.dtype)

    stages = [down, lambda k: second(1, k), lambda k: third(1, k), final]
    for step in range(len(stages) + last):
        for k in steps:
            if 0 <= step - k < len(stages):
                stages[step - k](k)

    for k in steps:
        for r in range(2):
            for copy in [copies_c[r][k], copies_b[r][k]] + copies_a[r][k]:
                copy.wait_send()
        for copy in gathers_a[k] + [gathers_b[k], gathers_c[k]]:
            copy.wait_send()


def local(
    residual,
    attention,
    out_weight,
    norm_gain,
    route_ids,
    route_weight,
    gate_weight,
    up_weight,
    down_weight,
):
    n = lax.axis_size("expert")
    rows, model = residual.shape
    width = model // PIECES
    hidden_units = gate_weight.shape[2]
    far = n // 4
    count = len(CHUNKS)
    bf16, f32 = jnp.bfloat16, jnp.float32
    vmem = pl.BlockSpec(memory_space=pltpu.VMEM)
    hbm = pl.BlockSpec(memory_space=pltpu.HBM)
    dma = pltpu.SemaphoreType.DMA
    return pl.pallas_call(
        functools.partial(kernel, n, FF_WIN // hidden_units),
        out_shape=jax.ShapeDtypeStruct((rows, model), bf16),
        in_specs=[vmem] * 5 + [hbm] * 4,
        out_specs=vmem,
        scratch_shapes=[
            pltpu.VMEM(out_weight.shape, bf16),
            pltpu.VMEM(gate_weight.shape[1:], bf16),
            pltpu.VMEM(up_weight.shape[1:], bf16),
            pltpu.VMEM(down_weight.shape[1:], bf16),
            pltpu.VMEM((2 * n, PIECES, width), f32),
            pltpu.VMEM((far, 2, 2, 2 * PIECES, width + META), bf16),
            pltpu.VMEM((2 * n, PIECES, width + META), f32),
            pltpu.VMEM((2, PIECES, width), f32),
            pltpu.VMEM((PIECES, width), f32),
            pltpu.VMEM((2, PIECES, META), f32),
            pltpu.VMEM((2, 2 * far, 2 * PIECES, width), bf16),
            pltpu.VMEM((2, 2 * far, 2 * PIECES, width), bf16),
            pltpu.VMEM((2, far, 2 * PIECES, width), bf16),
            pltpu.VMEM((2, far, 2 * PIECES, width), bf16),
            pltpu.VMEM((2, far - 1, 2 * PIECES, width), bf16),
            pltpu.VMEM((2, far - 1, 2 * PIECES, width), bf16),
            dma((4,)),
            dma((2, count, 2)),
            dma((2, count, 2)),
            dma((2, count, far - 1, 2)),
            dma((count, 2)),
            dma((count, 2)),
            dma((count, far - 1, 2)),
        ],
        compiler_params=pltpu.CompilerParams(
            collective_id=0, has_side_effects=True, vmem_limit_bytes=48 * 1024 * 1024
        ),
    )(
        residual,
        attention,
        norm_gain.reshape(1, model),
        route_ids,
        route_weight,
        out_weight,
        gate_weight,
        up_weight,
        down_weight,
    )


def solution(mesh):
    return jax.shard_map(
        local,
        mesh=mesh,
        in_specs=(
            P(("groups", "expert"), None),
            P("groups", "expert"),
            P("expert", None),
            P(),
            P(("groups", "expert"), None),
            P(("groups", "expert"), None),
            P("expert", None, None),
            P("expert", None, None),
            P("expert", None, None),
        ),
        out_specs=P(("groups", "expert"), None),
        check_vma=False,
    )
```

time: 161 us -> 47.9 us (0.30)
  waiting for transfers between devices: 93.6 us -> 0 us
  Pallas kernels: 0 us -> 39.8 us
  blocking collectives: 35 us -> 0 us
  between operations: 14.1 us -> 0.02 us
  matrix products: 13.1 us -> 0 us
  local copies, waits for them, and re-layouts: 3.03 us -> 7.7 us
  other arithmetic: 1.99 us -> 0 us
    unnamed x2 -> x0, waiting for transfers between devices: 93.6 us -> none
    pallas_call x0 -> x1, Pallas kernels: none -> 39.8 us  [local(): pl.pallas_call(functools.partial(kernel, n, FF_WIN // hidden_units), out_...]
    all_to_all x2 -> x0, blocking collectives: 35 us -> none  [the longest x1 18.1 us: local(): lax.all_to_all(copies, 'expert', split_axis=0, concat_axis=0, tiled=True)]
    dot_general x5 -> x0, matrix products: 13.1 us -> none  [the longest x1 5.25 us: expert_partial(): jnp.dot(activated, w_down[0], preferred_element_type=jnp.float32)]
    unnamed x13 -> x15, local copies, waits for them, and re-layouts: 2.05 us -> 7.7 us
    reduce_sum x4 -> x0, other arithmetic: 1.86 us -> none  [the longest x1 1.11 us: local(): jnp.mean(hidden_state * hidden_state, axis=-1, keepdims=True) + EPSILON]
  transfers between devices with their start and end apart: 1 -> 0, of which waited for: 1 -> 0; matrix products, arithmetic and copies ran while one was open for 1% -> 0% of each run, Pallas kernels for 0% -> 0%
where the time goes in v1:
time: 47.9 us; the launch traced here: 47.5 us
  Pallas kernels  39.8 us (83%)
  local copies, waits for them, and re-layouts  7.7 us (16%)
    pallas_call x1, Pallas kernels, local(): pl.pallas_call(functools.partial(kernel, n, FF_WIN // hidden_units), out_...  39.8 us
    unnamed x15, local copies, waits for them, and re-layouts  7.7 us

profile of v1, /device:TPU:0, one launch (start us, length us, event | category | flops | bytes accessed | tf_op | source)
XLA Modules:
  0.0 47.5 jit_solution(28187954699487552)
XLA Ops:
  0.0 0.0 copy-start
  0.0 2.0 %copy-done = bf16[1,7168,256]{2,1,0:T(8,128)(2,1)S(1)} copy-done((bf16[1,7168,256]{2,1,0:T(8,128)(2,1)S(1)}, bf16[1,7168,256]{2,1,0:T(8,128)(2,1)}, u32[]{:S(2)}) %copy-start) | copy-done | bytes 3670040
  2.0 0.0 copy-start.1
  2.0 1.5 %copy-done.1 = bf16[128,7168]{1,0:T(8,128)(2,1)S(1)} copy-done((bf16[128,7168]{1,0:T(8,128)(2,1)S(1)}, bf16[128,7168]{1,0:T(8,128)(2,1)}, u32[]{:S(2)}) %copy-start.1) | copy-done | bytes 1835032
  3.5 0.0 copy-start.2
  3.5 0.7 %copy-done.2 = bf16[2,7168]{1,0:T(2,128)(2,1)S(1)} copy-done((bf16[2,7168]{1,0:T(2,128)(2,1)S(1)}, bf16[2,7168]{1,0:T(2,128)(2,1)}, u32[]{:S(2)}) %copy-start.2) | copy-done | bytes 28696
  4.3 0.0 copy-start.3
  4.3 0.7 %copy-done.3 = f32[7168]{0:T(1024)S(1)} copy-done((f32[7168]{0:T(1024)S(1)}, f32[7168]{0:T(1024)}, u32[]{:S(2)}) %copy-start.3) | copy-done | bytes 28696
  5.0 0.0 copy-start.4
  5.0 0.7 %copy-done.4 = bf16[32,128]{1,0:T(8,128)(2,1)S(1)} copy-done((bf16[32,128]{1,0:T(8,128)(2,1)S(1)}, bf16[32,128]{1,0:T(8,128)(2,1)}, u32[]{:S(2)}) %copy-start.4) | copy-done | bytes 8216
  5.7 0.0 copy-start.5
  5.7 0.7 %copy-done.5 = s32[2,2]{1,0:T(2,128)S(1)} copy-done((s32[2,2]{1,0:T(2,128)S(1)}, s32[2,2]{1,0:T(2,128)}, u32[]{:S(2)}) %copy-start.5) | copy-done | bytes 40
  6.4 0.0 copy-start.6
  6.4 0.7 %copy-done.6 = f32[2,2]{1,0:T(2,128)S(1)} copy-done((f32[2,2]{1,0:T(2,128)S(1)}, f32[2,2]{1,0:T(2,128)}, u32[]{:S(2)}) %copy-start.6) | copy-done | bytes 40
  7.1 39.8 %shard_map.91 = bf16[2,7168]{1,0:T(2,128)(2,1)S(1)} custom-call(bf16[2,7168]{1,0:T(2,128)(2,1)S(1)} %copy-done.2, bf16[32,128]{1,0:T(8,128)(2,1)S(1)} %copy-done.4, f32[1,7168]{1,0:T(1,128)S(1)} %bitcast.1, s32[2,2]{1,0:T(2,128)S(1)} %copy-done.5, f32[2,2]{1,0:T(2,128)S(1)} %copy-done.6, bf16[128,7168]{1,0:T(8,128)(2,1)S(1)} %copy-done.1, ...), custom_call_target="tpu_custom_call" | custom-call | tf_op jit(solution)/shard_map/pallas_call | solution.py:371
  46.9 0.6 %copy.11 = bf16[2,7168]{1,0:T(2,128)(2,1)} copy(bf16[2,7168]{1,0:T(2,128)(2,1)S(1)} %shard_map.91) | data formatting | bytes 57344
Async XLA Ops:
  0.0 2.0 %copy-start = (bf16[1,7168,256]{2,1,0:T(8,128)(2,1)S(1)}, bf16[1,7168,256]{2,1,0:T(8,128)(2,1)}, u32[]{:S(2)}) copy-start(bf16[1,7168,256]{2,1,0:T(8,128)(2,1)} %wg_hbm.1) | copy-start | bytes 11010052
  2.0 1.5 %copy-start.1 = (bf16[128,7168]{1,0:T(8,128)(2,1)S(1)}, bf16[128,7168]{1,0:T(8,128)(2,1)}, u32[]{:S(2)}) copy-start(bf16[128,7168]{1,0:T(8,128)(2,1)} %wo_hbm.1) | copy-start | bytes 5505028
  3.5 0.7 %copy-start.2 = (bf16[2,7168]{1,0:T(2,128)(2,1)S(1)}, bf16[2,7168]{1,0:T(2,128)(2,1)}, u32[]{:S(2)}) copy-start(bf16[2,7168]{1,0:T(2,128)(2,1)} %residual.1) | copy-start | bytes 86020
  4.3 0.7 %copy-start.3 = (f32[7168]{0:T(1024)S(1)}, f32[7168]{0:T(1024)}, u32[]{:S(2)}) copy-start(f32[7168]{0:T(1024)} %param.12) | copy-start | bytes 86020
  5.0 0.7 %copy-start.4 = (bf16[32,128]{1,0:T(8,128)(2,1)S(1)}, bf16[32,128]{1,0:T(8,128)(2,1)}, u32[]{:S(2)}) copy-start(bf16[32,128]{1,0:T(8,128)(2,1)} %attention.1) | copy-start | bytes 24580
  5.7 0.7 %copy-start.5 = (s32[2,2]{1,0:T(2,128)S(1)}, s32[2,2]{1,0:T(2,128)}, u32[]{:S(2)}) copy-start(s32[2,2]{1,0:T(2,128)} %route_ids.1) | copy-start | bytes 52
  6.4 0.7 %copy-start.6 = (f32[2,2]{1,0:T(2,128)S(1)}, f32[2,2]{1,0:T(2,128)}, u32[]{:S(2)}) copy-start(f32[2,2]{1,0:T(2,128)} %route_weight.1) | copy-start | bytes 52

commit v2 on v1

--- a/solution.py
+++ b/solution.py
@@ -11,7 +11,7 @@
 EPSILON = 1e-06
 PIECES = 8
 META = 128
-CHUNKS = ((0, 512), (512, 384))
+CHUNKS = ((0, 896),)
 MESH = pl.DeviceIdType.MESH
 
 
@@ -25,16 +25,21 @@
 def kernel(
     n,
     expert_split,
+    residual_hbm,
+    attention_hbm,
+    gain_hbm,
+    ids_hbm,
+    weight_hbm,
+    wo_hbm,
+    wg_hbm,
+    wu_hbm,
+    wd_hbm,
+    out,
     residual,
     attention,
     gain,
     route_ids,
     route_weight,
-    wo_hbm,
-    wg_hbm,
-    wu_hbm,
-    wd_hbm,
-    out,
     wo,
     wg,
     wu,
@@ -45,7 +50,6 @@
     hidden,
     gain_tile,
     meta,
-    send_c,
     recv_c,
     send_b,
     recv_b,
@@ -69,14 +73,27 @@
     peer_c, peer_b = me + 1 - 2 * c, me + 2 - 4 * b
     peers_a = [lax.rem(me + 4 * d, n) for d in range(1, far)]
 
+    small = [
+        pltpu.make_async_copy(source, target, load_sem.at[4 + place])
+        for place, (source, target) in enumerate(
+            [
+                (attention_hbm, attention),
+                (residual_hbm, residual),
+                (gain_hbm, gain),
+                (ids_hbm, route_ids),
+                (weight_hbm, route_weight),
+            ]
+        )
+    ]
+    for load in small:
+        load.start()
     loads = [
         pltpu.make_async_copy(wo_hbm, wo, load_sem.at[0]),
         pltpu.make_async_copy(wg_hbm.at[0], wg, load_sem.at[1]),
         pltpu.make_async_copy(wu_hbm.at[0], wu, load_sem.at[2]),
         pltpu.make_async_copy(wd_hbm.at[0], wd, load_sem.at[3]),
     ]
-    for load in loads:
-        load.start()
+    loads[0].start()
 
     barrier = pltpu.get_barrier_semaphore()
     for peer in [peer_c, peer_b] + peers_a:
@@ -92,127 +109,76 @@
             device_id_type=MESH,
         )
 
-    def lanes(k):
-        return pl.ds(*CHUNKS[k])
-
-    def wide(k):
-        start, size = CHUNKS[k]
-        return pl.ds(start, size + (META if k == last else 0))
-
-    copies_c = [
-        [
-            remote(send_c.at[r, :, :, lanes(k)], recv_c.at[r, :, :, lanes(k)], c_sem.at[r, k], peer_c)
-            for k in steps
-        ]
-        for r in range(2)
-    ]
-    copies_b = [
-        [
-            remote(send_b.at[r, :, :, lanes(k)], recv_b.at[r, :, :, lanes(k)], b_sem.at[r, k], peer_b)
-            for k in steps
-        ]
-        for r in range(2)
-    ]
-    copies_a = [
-        [
-            [
-                remote(
-                    send_a.at[r, d, :, lanes(k)],
-                    recv_a.at[r, d, :, lanes(k)],
-                    a_sem.at[r, k, d],
-                    peers_a[d],
-                )
-                for d in range(far - 1)
-            ]
-            for k in steps
-        ]
-        for r in range(2)
-    ]
-    gathers_a = [
-        [
-            remote(
-                gathered.at[a, b, c, :, wide(k)],
-                gathered.at[a, b, c, :, wide(k)],
-                ga_sem.at[k, d],
-                peers_a[d],
+    half, quarter = n, n // 2
+    other_half, own_half = pl.ds((1 - c) * half, half), c * half
+    copies_c, copies_b, copies_a = [], [], []
+    for r in range(2):
+        copies_c.append([])
+        copies_b.append([])
+        copies_a.append([])
+        for k in steps:
+            copies_c[r].append(
+                remote(partial[r][k].at[other_half], recv_c[r][k], c_sem.at[r, k], peer_c)
             )
-            for d in range(far - 1)
-        ]
-        for k in steps
-    ]
-    gathers_b = [
-        remote(gathered.at[:, b, c, :, wide(k)], gathered.at[:, b, c, :, wide(k)], gb_sem.at[k], peer_b)
-        for k in steps
-    ]
-    gathers_c = [
-        remote(gathered.at[:, :, c, :, wide(k)], gathered.at[:, :, c, :, wide(k)], gc_sem.at[k], peer_c)
-        for k in steps
-    ]
-
-    def block(owner, k):
-        start, size = CHUNKS[k]
-        return partial[pl.ds(2 * owner, 2), :, start : start + size].reshape(2 * PIECES, size)
-
-    def keep(owner, k, value):
-        start, size = CHUNKS[k]
-        partial[pl.ds(2 * owner, 2), :, start : start + size] = value.reshape(2, PIECES, size)
-
-    def spread(k, left, right, scale):
+            copies_b[r].append(remote(send_b[r][k], recv_b[r][k], b_sem.at[r, k], peer_b))
+            copies_a[r].append(
+                [
+                    remote(send_a[r][k].at[d], recv_a[r][k].at[d], a_sem.at[r, k, d], peers_a[d])
+                    for d in range(far - 1)
+                ]
+            )
+    gathers_a, gathers_b, gathers_c = [], [], []
+    for k in steps:
+        own, row, plane = gathered[k].at[c, b, a], gathered[k].at[c, b], gathered[k].at[c]
+        gathers_a.append([remote(own, own, ga_sem.at[k, d], peers_a[d]) for d in range(far - 1)])
+        gathers_b.append(remote(row, row, gb_sem.at[k], peer_b))
+        gathers_c.append(remote(plane, plane, gc_sem.at[k], peer_c))
+
+    def spread(r, k, left, right, scale):
         start, size = CHUNKS[k]
         for j in range(PIECES):
             at = j * width + start
             product = jnp.dot(left, right[:, at : at + size], preferred_element_type=jnp.float32)
-            partial[:, j, start : start + size] = product if scale is None else product * scale
-
-    def first(r, k):
-        start, size = CHUNKS[k]
-
-        @pl.loop(0, 2 * far)
-        def _(i):
-            value = block(2 * i + 1 - c, k).astype(jnp.bfloat16)
-            send_c[r, i, :, start : start + size] = value
+            partial[r][k][:, j, :] = product if scale is None else product * scale
 
     def second(r, k):
-        start, size = CHUNKS[k]
+        size = CHUNKS[k][1]
         copies_c[r][k].wait_recv()
-
-        def total(i):
-            received = recv_c[r, i, :, start : start + size].astype(jnp.float32)
-            return block(2 * i + c, k) + received
-
-        @pl.loop(0, far)
-        def _(q):
-            send_b[r, q, :, start : start + size] = total(2 * q + 1 - b).astype(jnp.bfloat16)
-
+        at = (1 - b) * quarter
+        total = partial[r][k][pl.ds(own_half + at, quarter)] + recv_c[r][k][pl.ds(at, quarter)]
+        send_b[r][k][...] = total.reshape(far, 2 * PIECES, size).astype(jnp.bfloat16)
         copies_b[r][k].start()
 
-        @pl.loop(0, far)
-        def _(q):
-            i = 2 * q + b
-            keep(2 * i + c, k, total(i))
-
     def third(r, k):
-        start, size = CHUNKS[k]
+        size = CHUNKS[k][1]
         copies_b[r][k].wait_recv()
-
-        def total(q):
-            received = recv_b[r, q, :, start : start + size].astype(jnp.float32)
-            return block(4 * q + 2 * b + c, k) + received
-
         for d in range(far - 1):
-            value = total(peers_a[d] // 4).astype(jnp.bfloat16)
-            send_a[r, d, :, start : start + size] = value
+            q = peers_a[d] // 4
+            at = b * quarter + 2 * q
+            total = partial[r][k][pl.ds(own_half + at, 2)] + recv_c[r][k][pl.ds(at, 2)]
+            total = total.reshape(2 * PIECES, size) + recv_b[r][k][q].astype(jnp.float32)
+            send_a[r][k][d] = total.astype(jnp.bfloat16)
             copies_a[r][k][d].start()
-        keep(me, k, total(a))
 
     def fourth(r, k):
-        start, size = CHUNKS[k]
-        value = block(me, k)
+        size = CHUNKS[k][1]
+        at = b * quarter + 2 * a
+        total = partial[r][k][pl.ds(own_half + at, 2)] + recv_c[r][k][pl.ds(at, 2)]
+        total = total.reshape(2 * PIECES, size) + recv_b[r][k][a].astype(jnp.float32)
         for d in range(far - 1):
             copies_a[r][k][d].wait_recv()
-            value = value + recv_a[r, d, :, start : start + size].astype(jnp.float32)
-        return value.reshape(2, PIECES, size)
-
+            total = total + recv_a[r][k][d].astype(jnp.float32)
+        return total.reshape(2, PIECES, size)
+
+    for load in small:
+        load.wait()
+    place = lax.broadcasted_iota(jnp.int32, (2 * n, 2 * n), 0)
+    token = lax.broadcasted_iota(jnp.int32, (2 * n, 2 * n), 1)
+    bits = quarter.bit_length() - 1
+    source = ((place & (quarter - 1)) >> 1) * 8 + ((place >> bits) & 1) * 4
+    source = source + (place >> (bits + 1)) * 2 + (place & 1)
+    order = jnp.where(source == token, 1.0, 0.0).astype(jnp.bfloat16)
+    heads = jnp.dot(order, attention[...], preferred_element_type=jnp.float32).astype(jnp.bfloat16)
     lane = lax.broadcasted_iota(jnp.int32, (1, META), 1)
     meta[...] = jnp.zeros_like(meta)
     for row in range(2):
@@ -233,9 +199,7 @@
         value = hidden[:, :, start : start + size] + fourth(0, k)
         hidden[:, :, start : start + size] = value
         scaled = value * gain_tile[:, start : start + size][None]
-        gathered[a, b, c, :, start : start + size] = scaled.reshape(2 * PIECES, size).astype(
-            jnp.bfloat16
-        )
+        gathered[k][c, b, a, :, :size] = scaled.reshape(2 * PIECES, size).astype(jnp.bfloat16)
         part = jnp.sum(jnp.sum(value * value, axis=2, keepdims=True), axis=1, keepdims=True)
         squares.append(part)
         if k == last:
@@ -244,7 +208,7 @@
                 spreaded = jnp.broadcast_to(total[row], (1, META))
                 for place, piece in enumerate(split_three(spreaded)):
                     meta[row, place : place + 1, :] = piece
-            gathered[a, b, c, :, width:] = meta[...].reshape(2 * PIECES, META).astype(jnp.bfloat16)
+            gathered[k][c, b, a, :, size:] = meta[...].reshape(2 * PIECES, META).astype(jnp.bfloat16)
         for copy in gathers_a[k]:
             copy.start()
 
@@ -264,10 +228,10 @@
         size_wide = size + (META if k == last else 0)
         gathers_c[k].wait_recv()
 
-        @pl.loop(0, n)
-        def _(owner):
-            value = gathered[owner // 4, (owner // 2) % 2, owner % 2, :, start : start + size_wide]
-            tokens[pl.ds(2 * owner, 2), :, start : start + size_wide] = value.astype(
+        @pl.loop(0, n, unroll=4)
+        def _(i):
+            value = gathered[k][i // (2 * far), (i // far) % 2, i % far]
+            tokens[pl.ds(2 * i, 2), :, start : start + size_wide] = value.astype(
                 jnp.float32
             ).reshape(2, PIECES, size_wide)
 
@@ -290,8 +254,9 @@
     def project(k):
         if k == 0:
             loads[0].wait()
-        spread(k, attention[...], wo, None)
-        first(0, k)
+            for load in loads[1:]:
+                load.start()
+        spread(0, k, heads, wo, None)
         if k == 0:
             pl.semaphore_wait(barrier, far + 1)
         copies_c[0][k].start()
@@ -322,8 +287,7 @@
     loads[3].wait()
 
     def down(k):
-        spread(k, act, wd, coef)
-        first(1, k)
+        spread(1, k, act, wd, coef)
         copies_c[1][k].start()
 
     def final(k):
@@ -364,6 +328,7 @@
     hidden_units = gate_weight.shape[2]
     far = n // 4
     count = len(CHUNKS)
+    sizes = [size for _, size in CHUNKS]
     bf16, f32 = jnp.bfloat16, jnp.float32
     vmem = pl.BlockSpec(memory_space=pltpu.VMEM)
     hbm = pl.BlockSpec(memory_space=pltpu.HBM)
@@ -371,26 +336,33 @@
     return pl.pallas_call(
         functools.partial(kernel, n, FF_WIN // hidden_units),
         out_shape=jax.ShapeDtypeStruct((rows, model), bf16),
-        in_specs=[vmem] * 5 + [hbm] * 4,
+        in_specs=[hbm] * 9,
         out_specs=vmem,
         scratch_shapes=[
+            pltpu.VMEM(residual.shape, bf16),
+            pltpu.VMEM(attention.shape, bf16),
+            pltpu.VMEM((1, model), f32),
+            pltpu.VMEM(route_ids.shape, jnp.int32),
+            pltpu.VMEM(route_weight.shape, f32),
             pltpu.VMEM(out_weight.shape, bf16),
             pltpu.VMEM(gate_weight.shape[1:], bf16),
             pltpu.VMEM(up_weight.shape[1:], bf16),
             pltpu.VMEM(down_weight.shape[1:], bf16),
-            pltpu.VMEM((2 * n, PIECES, width), f32),
-            pltpu.VMEM((far, 2, 2, 2 * PIECES, width + META), bf16),
+            [[pltpu.VMEM((2 * n, PIECES, size), f32) for size in sizes] for _ in range(2)],
+            [
+                pltpu.VMEM((2, 2, far, 2 * PIECES, size + META * (k == count - 1)), bf16)
+                for k, size in enumerate(sizes)
+            ],
             pltpu.VMEM((2 * n, PIECES, width + META), f32),
             pltpu.VMEM((2, PIECES, width), f32),
             pltpu.VMEM((PIECES, width), f32),
             pltpu.VMEM((2, PIECES, META), f32),
-            pltpu.VMEM((2, 2 * far, 2 * PIECES, width), bf16),
-            pltpu.VMEM((2, 2 * far, 2 * PIECES, width), bf16),
-            pltpu.VMEM((2, far, 2 * PIECES, width), bf16),
-            pltpu.VMEM((2, far, 2 * PIECES, width), bf16),
-            pltpu.VMEM((2, far - 1, 2 * PIECES, width), bf16),
-            pltpu.VMEM((2, far - 1, 2 * PIECES, width), bf16),
-            dma((4,)),
+            [[pltpu.VMEM((n, PIECES, size), f32) for size in sizes] for _ in range(2)],
+            [[pltpu.VMEM((far, 2 * PIECES, size), bf16) for size in sizes] for _ in range(2)],
+            [[pltpu.VMEM((far, 2 * PIECES, size), bf16) for size in sizes] for _ in range(2)],
+            [[pltpu.VMEM((far - 1, 2 * PIECES, size), bf16) for size in sizes] for _ in range(2)],
+            [[pltpu.VMEM((far - 1, 2 * PIECES, size), bf16) for size in sizes] for _ in range(2)],
+            dma((9,)),
             dma((2, count, 2)),
             dma((2, count, 2)),
             dma((2, count, far - 1, 2)),
@@ -399,7 +371,7 @@
             dma((count, far - 1, 2)),
         ],
         compiler_params=pltpu.CompilerParams(
-            collective_id=0, has_side_effects=True, vmem_limit_bytes=48 * 1024 * 1024
+            collective_id=0, has_side_effects=True, vmem_limit_bytes=60 * 1024 * 1024
         ),
     )(
         residual,

time: 47.9 us -> 40.1 us (0.84)
  local copies, waits for them, and re-layouts: 7.7 us -> 1.38 us
  Pallas kernels: 39.8 us -> 38.5 us
    unnamed x15 -> x1, local copies, waits for them, and re-layouts: 7.7 us -> 1.38 us
    pallas_call x1, Pallas kernels: 39.8 us -> 38.5 us  [local(): pl.pallas_call(functools.partial(kernel, n, FF_WIN // hidden_units), out_...]
where the time goes in v2:
time: 40.1 us; the launch traced here: 39.9 us
  Pallas kernels  38.5 us (96%)
  local copies, waits for them, and re-layouts  1.38 us (3%)
    pallas_call x1, Pallas kernels, local(): pl.pallas_call(functools.partial(kernel, n, FF_WIN // hidden_units), out_...  38.5 us
    unnamed x1, local copies, waits for them, and re-layouts  1.38 us

profile of v2, /device:TPU:0, one launch (start us, length us, event | category | flops | bytes accessed | tf_op | source)
XLA Modules:
  0.0 39.9 jit_solution(6418809565854771972)
XLA Ops:
  0.0 38.5 %shard_map.91 = bf16[2,7168]{1,0:T(2,128)(2,1)} custom-call(bf16[2,7168]{1,0:T(2,128)(2,1)} %residual_hbm.1, bf16[32,128]{1,0:T(8,128)(2,1)} %attention_hbm.1, f32[1,7168]{1,0:T(1,128)} %bitcast.1, s32[2,2]{1,0:T(2,128)} %ids_hbm.1, f32[2,2]{1,0:T(2,128)} %weight_hbm.1, bf16[128,7168]{1,0:T(8,128)(2,1)} %wo_hbm.1, bf16[1,7168,256]{2,1,0:T(8,128)(2,1)} %wg_hbm.1, ...), custom_call_target="tpu_custom_call" | custom-call | tf_op jit(solution)/shard_map/pallas_call | solution.py:336
  38.6 1.4 %copy.11 = bf16[2,7168]{1,0:T(2,128)(2,1)} copy(bf16[2,7168]{1,0:T(2,128)(2,1)} %shard_map.91) | data formatting | bytes 57344

commit v3 on v2

--- a/solution.py
+++ b/solution.py
@@ -51,27 +51,23 @@
     gain_tile,
     meta,
     recv_c,
-    send_b,
-    recv_b,
     send_a,
     recv_a,
     load_sem,
     c_sem,
-    b_sem,
     a_sem,
     gc_sem,
-    gb_sem,
     ga_sem,
 ):
     width = gain_tile.shape[1]
-    far = n // 4
     top = route_ids.shape[1]
     steps = range(len(CHUNKS))
     last = len(CHUNKS) - 1
     me = lax.axis_index("expert")
-    a, b, c = me // 4, (me // 2) % 2, me % 2
-    peer_c, peer_b = me + 1 - 2 * c, me + 2 - 4 * b
-    peers_a = [lax.rem(me + 4 * d, n) for d in range(1, far)]
+    c = me % 2
+    peer_c = me + 1 - 2 * c
+    chips = n // 2
+    peers = [lax.rem(me + 2 * d, n) for d in range(1, chips)]
 
     small = [
         pltpu.make_async_copy(source, target, load_sem.at[4 + place])
@@ -96,7 +92,7 @@
     loads[0].start()
 
     barrier = pltpu.get_barrier_semaphore()
-    for peer in [peer_c, peer_b] + peers_a:
+    for peer in [peer_c] + peers:
         pl.semaphore_signal(barrier, inc=1, device_id={"expert": peer}, device_id_type=MESH)
 
     def remote(src, dst, sems, peer):
@@ -109,29 +105,25 @@
             device_id_type=MESH,
         )
 
-    half, quarter = n, n // 2
-    other_half, own_half = pl.ds((1 - c) * half, half), c * half
-    copies_c, copies_b, copies_a = [], [], []
+    other_half, own_half = pl.ds((1 - c) * n, n), c * n
+    copies_c, copies_a = [], []
     for r in range(2):
         copies_c.append([])
-        copies_b.append([])
         copies_a.append([])
         for k in steps:
             copies_c[r].append(
                 remote(partial[r][k].at[other_half], recv_c[r][k], c_sem.at[r, k], peer_c)
             )
-            copies_b[r].append(remote(send_b[r][k], recv_b[r][k], b_sem.at[r, k], peer_b))
             copies_a[r].append(
                 [
-                    remote(send_a[r][k].at[d], recv_a[r][k].at[d], a_sem.at[r, k, d], peers_a[d])
-                    for d in range(far - 1)
+                    remote(send_a[r][k].at[d], recv_a[r][k].at[d], a_sem.at[r, k, d], peers[d])
+                    for d in range(chips - 1)
                 ]
             )
-    gathers_a, gathers_b, gathers_c = [], [], []
+    gathers_a, gathers_c = [], []
     for k in steps:
-        own, row, plane = gathered[k].at[c, b, a], gathered[k].at[c, b], gathered[k].at[c]
-        gathers_a.append([remote(own, own, ga_sem.at[k, d], peers_a[d]) for d in range(far - 1)])
-        gathers_b.append(remote(row, row, gb_sem.at[k], peer_b))
+        own, plane = gathered[k].at[c, me // 2], gathered[k].at[c]
+        gathers_a.append([remote(own, own, ga_sem.at[k, d], peers[d]) for d in range(chips - 1)])
         gathers_c.append(remote(plane, plane, gc_sem.at[k], peer_c))
 
     def spread(r, k, left, right, scale):
@@ -141,42 +133,30 @@
             product = jnp.dot(left, right[:, at : at + size], preferred_element_type=jnp.float32)
             partial[r][k][:, j, :] = product if scale is None else product * scale
 
+    def pair_sum(r, k, owner):
+        at = 2 * (owner // 2)
+        total = partial[r][k][pl.ds(own_half + at, 2)] + recv_c[r][k][pl.ds(at, 2)]
+        return total.reshape(2 * PIECES, CHUNKS[k][1])
+
     def second(r, k):
-        size = CHUNKS[k][1]
         copies_c[r][k].wait_recv()
-        at = (1 - b) * quarter
-        total = partial[r][k][pl.ds(own_half + at, quarter)] + recv_c[r][k][pl.ds(at, quarter)]
-        send_b[r][k][...] = total.reshape(far, 2 * PIECES, size).astype(jnp.bfloat16)
-        copies_b[r][k].start()
+        for d in range(chips - 1):
+            send_a[r][k][d] = pair_sum(r, k, peers[d]).astype(jnp.bfloat16)
+            copies_a[r][k][d].start()
 
     def third(r, k):
-        size = CHUNKS[k][1]
-        copies_b[r][k].wait_recv()
-        for d in range(far - 1):
-            q = peers_a[d] // 4
-            at = b * quarter + 2 * q
-            total = partial[r][k][pl.ds(own_half + at, 2)] + recv_c[r][k][pl.ds(at, 2)]
-            total = total.reshape(2 * PIECES, size) + recv_b[r][k][q].astype(jnp.float32)
-            send_a[r][k][d] = total.astype(jnp.bfloat16)
-            copies_a[r][k][d].start()
-
-    def fourth(r, k):
-        size = CHUNKS[k][1]
-        at = b * quarter + 2 * a
-        total = partial[r][k][pl.ds(own_half + at, 2)] + recv_c[r][k][pl.ds(at, 2)]
-        total = total.reshape(2 * PIECES, size) + recv_b[r][k][a].astype(jnp.float32)
-        for d in range(far - 1):
+        total = pair_sum(r, k, me)
+        for d in range(chips - 1):
             copies_a[r][k][d].wait_recv()
             total = total + recv_a[r][k][d].astype(jnp.float32)
-        return total.reshape(2, PIECES, size)
+        return total.reshape(2, PIECES, CHUNKS[k][1])
 
     for load in small:
         load.wait()
     place = lax.broadcasted_iota(jnp.int32, (2 * n, 2 * n), 0)
     token = lax.broadcasted_iota(jnp.int32, (2 * n, 2 * n), 1)
-    bits = quarter.bit_length() - 1
-    source = ((place & (quarter - 1)) >> 1) * 8 + ((place >> bits) & 1) * 4
-    source = source + (place >> (bits + 1)) * 2 + (place & 1)
+    bits = n.bit_length() - 1
+    source = ((place & (n - 1)) >> 1) * 4 + (place >> bits) * 2 + (place & 1)
     order = jnp.where(source == token, 1.0, 0.0).astype(jnp.bfloat16)
     heads = jnp.dot(order, attention[...], preferred_element_type=jnp.float32).astype(jnp.bfloat16)
     lane = lax.broadcasted_iota(jnp.int32, (1, META), 1)
@@ -196,10 +176,10 @@
 
     def normed(k):
         start, size = CHUNKS[k]
-        value = hidden[:, :, start : start + size] + fourth(0, k)
+        value = hidden[:, :, start : start + size] + third(0, k)
         hidden[:, :, start : start + size] = value
         scaled = value * gain_tile[:, start : start + size][None]
-        gathered[k][c, b, a, :, :size] = scaled.reshape(2 * PIECES, size).astype(jnp.bfloat16)
+        gathered[k][c, me // 2, :, :size] = scaled.reshape(2 * PIECES, size).astype(jnp.bfloat16)
         part = jnp.sum(jnp.sum(value * value, axis=2, keepdims=True), axis=1, keepdims=True)
         squares.append(part)
         if k == last:
@@ -208,17 +188,13 @@
                 spreaded = jnp.broadcast_to(total[row], (1, META))
                 for place, piece in enumerate(split_three(spreaded)):
                     meta[row, place : place + 1, :] = piece
-            gathered[k][c, b, a, :, size:] = meta[...].reshape(2 * PIECES, META).astype(jnp.bfloat16)
+            gathered[k][c, me // 2, :, size:] = meta[...].reshape(2 * PIECES, META).astype(jnp.bfloat16)
         for copy in gathers_a[k]:
             copy.start()
 
-    def pass_b(k):
+    def pass_on(k):
         for copy in gathers_a[k]:
             copy.wait_recv()
-        gathers_b[k].start()
-
-    def pass_c(k):
-        gathers_b[k].wait_recv()
         gathers_c[k].start()
 
     products = []
@@ -230,7 +206,7 @@
 
         @pl.loop(0, n, unroll=4)
         def _(i):
-            value = gathered[k][i // (2 * far), (i // far) % 2, i % far]
+            value = gathered[k][i // chips, i % chips]
             tokens[pl.ds(2 * i, 2), :, start : start + size_wide] = value.astype(
                 jnp.float32
             ).reshape(2, PIECES, size_wide)
@@ -258,16 +234,14 @@
                 load.start()
         spread(0, k, heads, wo, None)
         if k == 0:
-            pl.semaphore_wait(barrier, far + 1)
+            pl.semaphore_wait(barrier, chips)
         copies_c[0][k].start()
 
     stages = [
         project,
         lambda k: second(0, k),
-        lambda k: third(0, k),
         normed,
-        pass_b,
-        pass_c,
+        pass_on,
         consume,
     ]
     for step in range(len(stages) + last):
@@ -292,12 +266,12 @@
 
     def final(k):
         start, size = CHUNKS[k]
-        hidden[:, :, start : start + size] = hidden[:, :, start : start + size] + fourth(1, k)
+        hidden[:, :, start : start + size] = hidden[:, :, start : start + size] + third(1, k)
         for j in range(PIECES):
             at = j * width + start
             out[:, at : at + size] = hidden[:, j, start : start + size].astype(out.dtype)
 
-    stages = [down, lambda k: second(1, k), lambda k: third(1, k), final]
+    stages = [down, lambda k: second(1, k), final]
     for step in range(len(stages) + last):
         for k in steps:
             if 0 <= step - k < len(stages):
@@ -305,9 +279,9 @@
 
     for k in steps:
         for r in range(2):
-            for copy in [copies_c[r][k], copies_b[r][k]] + copies_a[r][k]:
+            for copy in [copies_c[r][k]] + copies_a[r][k]:
                 copy.wait_send()
-        for copy in gathers_a[k] + [gathers_b[k], gathers_c[k]]:
+        for copy in gathers_a[k] + [gathers_c[k]]:
             copy.wait_send()
 
 
@@ -326,7 +300,7 @@
     rows, model = residual.shape
     width = model // PIECES
     hidden_units = gate_weight.shape[2]
-    far = n // 4
+    chips = n // 2
     count = len(CHUNKS)
     sizes = [size for _, size in CHUNKS]
     bf16, f32 = jnp.bfloat16, jnp.float32
@@ -350,7 +324,7 @@
             pltpu.VMEM(down_weight.shape[1:], bf16),
             [[pltpu.VMEM((2 * n, PIECES, size), f32) for size in sizes] for _ in range(2)],
             [
-                pltpu.VMEM((2, 2, far, 2 * PIECES, size + META * (k == count - 1)), bf16)
+                pltpu.VMEM((2, chips, 2 * PIECES, size + META * (k == count - 1)), bf16)
                 for k, size in enumerate(sizes)
             ],
             pltpu.VMEM((2 * n, PIECES, width + META), f32),
@@ -358,17 +332,13 @@
             pltpu.VMEM((PIECES, width), f32),
             pltpu.VMEM((2, PIECES, META), f32),
             [[pltpu.VMEM((n, PIECES, size), f32) for size in sizes] for _ in range(2)],
-            [[pltpu.VMEM((far, 2 * PIECES, size), bf16) for size in sizes] for _ in range(2)],
-            [[pltpu.VMEM((far, 2 * PIECES, size), bf16) for size in sizes] for _ in range(2)],
-            [[pltpu.VMEM((far - 1, 2 * PIECES, size), bf16) for size in sizes] for _ in range(2)],
-            [[pltpu.VMEM((far - 1, 2 * PIECES, size), bf16) for size in sizes] for _ in range(2)],
+            [[pltpu.VMEM((chips - 1, 2 * PIECES, size), bf16) for size in sizes] for _ in range(2)],
+            [[pltpu.VMEM((chips - 1, 2 * PIECES, size), bf16) for size in sizes] for _ in range(2)],
             dma((9,)),
             dma((2, count, 2)),
-            dma((2, count, 2)),
-            dma((2, count, far - 1, 2)),
+            dma((2, count, chips - 1, 2)),
             dma((count, 2)),
-            dma((count, 2)),
-            dma((count, far - 1, 2)),
+            dma((count, chips - 1, 2)),
         ],
         compiler_params=pltpu.CompilerParams(
             collective_id=0, has_side_effects=True, vmem_limit_bytes=60 * 1024 * 1024

time: 40.1 us -> 34.8 us (0.87)
  Pallas kernels: 38.5 us -> 33.2 us
    pallas_call x1, Pallas kernels: 38.5 us -> 33.2 us  [local(): pl.pallas_call(functools.partial(kernel, n, FF_WIN // hidden_units), out_...]
where the time goes in v3:
time: 34.8 us; the launch traced here: 34.6 us
  Pallas kernels  33.2 us (95%)
  local copies, waits for them, and re-layouts  1.38 us (4%)
    pallas_call x1, Pallas kernels, local(): pl.pallas_call(functools.partial(kernel, n, FF_WIN // hidden_units), out_...  33.2 us
    unnamed x1, local copies, waits for them, and re-layouts  1.38 us

profile of v3, /device:TPU:0, one launch (start us, length us, event | category | flops | bytes accessed | tf_op | source)
XLA Modules:
  0.0 34.6 jit_solution(10918062827164513570)
XLA Ops:
  0.0 33.2 %shard_map.91 = bf16[2,7168]{1,0:T(2,128)(2,1)} custom-call(bf16[2,7168]{1,0:T(2,128)(2,1)} %residual_hbm.1, bf16[32,128]{1,0:T(8,128)(2,1)} %attention_hbm.1, f32[1,7168]{1,0:T(1,128)} %bitcast.1, s32[2,2]{1,0:T(2,128)} %ids_hbm.1, f32[2,2]{1,0:T(2,128)} %weight_hbm.1, bf16[128,7168]{1,0:T(8,128)(2,1)} %wo_hbm.1, bf16[1,7168,256]{2,1,0:T(8,128)(2,1)} %wg_hbm.1, ...), custom_call_target="tpu_custom_call" | custom-call | tf_op jit(solution)/shard_map/pallas_call | solution.py:310
  33.2 1.4 %copy.11 = bf16[2,7168]{1,0:T(2,128)(2,1)} copy(bf16[2,7168]{1,0:T(2,128)(2,1)} %shard_map.91) | data formatting | bytes 57344

commit v4 on v3

--- a/solution.py
+++ b/solution.py
@@ -89,7 +89,8 @@
         pltpu.make_async_copy(wu_hbm.at[0], wu, load_sem.at[2]),
         pltpu.make_async_copy(wd_hbm.at[0], wd, load_sem.at[3]),
     ]
-    loads[0].start()
+    for load in loads:
+        load.start()
 
     barrier = pltpu.get_barrier_semaphore()
     for peer in [peer_c] + peers:
@@ -120,11 +121,15 @@
                     for d in range(chips - 1)
                 ]
             )
+    sources = [lax.rem(me // 2 + chips - d, chips) for d in range(chips)]
     gathers_a, gathers_c = [], []
     for k in steps:
-        own, plane = gathered[k].at[c, me // 2], gathered[k].at[c]
+        own = gathered[k].at[c, me // 2]
         gathers_a.append([remote(own, own, ga_sem.at[k, d], peers[d]) for d in range(chips - 1)])
-        gathers_c.append(remote(plane, plane, gc_sem.at[k], peer_c))
+        blocks = [gathered[k].at[c, place] for place in sources]
+        gathers_c.append(
+            [remote(blocks[d], blocks[d], gc_sem.at[k, d], peer_c) for d in range(chips)]
+        )
 
     def spread(r, k, left, right, scale):
         start, size = CHUNKS[k]
@@ -191,26 +196,30 @@
             gathered[k][c, me // 2, :, size:] = meta[...].reshape(2 * PIECES, META).astype(jnp.bfloat16)
         for copy in gathers_a[k]:
             copy.start()
+        gathers_c[k][0].start()
 
     def pass_on(k):
-        for copy in gathers_a[k]:
-            copy.wait_recv()
-        gathers_c[k].start()
+        widen(k, c, sources[0])
+        for d in range(1, chips):
+            gathers_a[k][d - 1].wait_recv()
+            gathers_c[k][d].start()
+            widen(k, c, sources[d])
+
+    def widen(k, core, place):
+        start, size = CHUNKS[k]
+        size_wide = size + (META if k == last else 0)
+        value = gathered[k][core, place].astype(jnp.float32)
+        tokens[pl.ds(2 * (core * chips + place), 2), :, start : start + size_wide] = value.reshape(
+            2, PIECES, size_wide
+        )
 
     products = []
 
     def consume(k):
         start, size = CHUNKS[k]
-        size_wide = size + (META if k == last else 0)
-        gathers_c[k].wait_recv()
-
-        @pl.loop(0, n, unroll=4)
-        def _(i):
-            value = gathered[k][i // chips, i % chips]
-            tokens[pl.ds(2 * i, 2), :, start : start + size_wide] = value.astype(
-                jnp.float32
-            ).reshape(2, PIECES, size_wide)
-
+        for d in range(chips):
+            gathers_c[k][d].wait_recv()
+            widen(k, 1 - c, sources[d])
         if k == 0:
             loads[1].wait()
             loads[2].wait()
@@ -230,8 +239,6 @@
     def project(k):
         if k == 0:
             loads[0].wait()
-            for load in loads[1:]:
-                load.start()
         spread(0, k, heads, wo, None)
         if k == 0:
             pl.semaphore_wait(barrier, chips)
@@ -281,7 +288,7 @@
         for r in range(2):
             for copy in [copies_c[r][k]] + copies_a[r][k]:
                 copy.wait_send()
-        for copy in gathers_a[k] + [gathers_c[k]]:
+        for copy in gathers_a[k] + gathers_c[k]:
             copy.wait_send()
 
 
@@ -337,7 +344,7 @@
             dma((9,)),
             dma((2, count, 2)),
             dma((2, count, chips - 1, 2)),
-            dma((count, 2)),
+            dma((count, chips, 2)),
             dma((count, chips - 1, 2)),
         ],
         compiler_params=pltpu.CompilerParams(

time: 34.8 us -> 34.6 us (level)
  no operation moved by 1% of the time
where the time goes in v4:
time: 34.6 us; the launch traced here: 34.4 us
  Pallas kernels  33 us (95%)
  local copies, waits for them, and re-layouts  1.38 us (4%)
    pallas_call x1, Pallas kernels, local(): pl.pallas_call(functools.partial(kernel, n, FF_WIN // hidden_units), out_...  33 us
    unnamed x1, local copies, waits for them, and re-layouts  1.38 us

profile of v4, /device:TPU:0, one launch (start us, length us, event | category | flops | bytes accessed | tf_op | source)
XLA Modules:
  0.0 34.4 jit_solution(8384147889827372755)
XLA Ops:
  0.0 33.0 %shard_map.91 = bf16[2,7168]{1,0:T(2,128)(2,1)} custom-call(bf16[2,7168]{1,0:T(2,128)(2,1)} %residual_hbm.1, bf16[32,128]{1,0:T(8,128)(2,1)} %attention_hbm.1, f32[1,7168]{1,0:T(1,128)} %bitcast.1, s32[2,2]{1,0:T(2,128)} %ids_hbm.1, f32[2,2]{1,0:T(2,128)} %weight_hbm.1, bf16[128,7168]{1,0:T(8,128)(2,1)} %wo_hbm.1, bf16[1,7168,256]{2,1,0:T(8,128)(2,1)} %wg_hbm.1, ...), custom_call_target="tpu_custom_call" | custom-call | tf_op jit(solution)/shard_map/pallas_call | solution.py:317
  33.0 1.4 %copy.11 = bf16[2,7168]{1,0:T(2,128)(2,1)} copy(bf16[2,7168]{1,0:T(2,128)(2,1)} %shard_map.91) | data formatting | bytes 57344
